TPU v7x, 32 devices: a whole 2x2x4 slice. The times are simulated.
32 devices in a mesh: dp: 8 (over z, y), ctx: 4 (over x, core).
Axes of the slice: x: 2, y: 2, z: 4, core: 2. Of those that a mesh axis runs over, the one named last changes fastest.
Arguments:
- layer_input: bfloat16 [8, 1024, 8192], P('dp', 'ctx'), may hold values from -0.078125 to 0.078125
- query_rows: bfloat16 [8, 1024, 1024], P('dp', 'ctx'), may hold values from -6 to 6
- key_rows: bfloat16 [8, 1024, 128], P('dp', 'ctx'), may hold values from -6 to 6
- value_rows: bfloat16 [8, 1024, 128], P('dp', 'ctx'), may hold values from -6 to 6
- attn_out: bfloat16 [8, 1024, 1024], P('dp', 'ctx'), may hold values from -6 to 6
- d_attn: bfloat16 [8, 1024, 1024], P('dp', 'ctx'), may hold values from -6 to 6
- log_sum_exp: float32 [8, 8, 1024], P('dp', None, 'ctx')
- block_order: int32 [8], replicated, may hold values from 0 to 7, as said below
Outputs:
- d_query: bfloat16 [8, 1024, 1024], P('dp', 'ctx')
- d_weight: float32 [8192, 256], P(('dp', 'ctx'))
Inputs may be any that keep to these rules, and one draw needn't show every extreme that they name: `block_order`: each value appears exactly once.
All inputs are finite; a program needn't handle non-finite values.
Results may differ from a plain program's by a relative error of at most 0.0051.
Values may be sent and summed in bfloat16 or wider, within the bound.
A program may use at most 64 MiB of HBM per device.

v0:
```python
import jax
import jax.numpy as jnp
from jax import lax
from jax.sharding import PartitionSpec as P


def passed_along(value, axis, steps):
    count = lax.axis_size(axis)
    pairs = [(source, (source + steps) % count) for source in range(count)]
    return lax.ppermute(value, axis, pairs)


def slot_positions(block_order, owner, half):
    firsts = lax.dynamic_slice_in_dim(block_order, 2 * owner, 2)
    offsets = jnp.arange(half, dtype=jnp.int32)
    return (firsts[:, None] * half + offsets[None, :]).reshape(2 * half)


def body(layer_input, query_rows, key_rows, value_rows, attn_out, d_attn, log_sum_exp, block_order):
    rows = query_rows.shape[1]
    head_dim = key_rows.shape[2]
    heads = query_rows.shape[2] // head_dim
    half = rows // 2
    scale = head_dim ** (-0.5)
    width = lax.axis_size("ctx")
    mine = lax.axis_index("ctx")
    q_pos = slot_positions(block_order, mine, half)
    queries = query_rows[0].reshape(rows, heads, head_dim)
    grad_out = d_attn[0].reshape(rows, heads, head_dim)
    saved = attn_out[0].reshape(rows, heads, head_dim)
    delta = jnp.sum(grad_out.astype(jnp.float32) * saved.astype(jnp.float32), axis=2).T
    stats = log_sum_exp[0]

    def tile(pair, k_pos):
        keys = pair[0]
        values = pair[1]
        score = jnp.einsum("rhd,sd->hrs", queries, keys, preferred_element_type=jnp.float32) * scale
        visible = q_pos[:, None] >= k_pos[None, :]
        prob = jnp.where(visible[None], jnp.exp(score - stats[:, :, None]), 0.0)
        d_value = jnp.einsum(
            "hrs,rhd->sd", prob.astype(jnp.bfloat16), grad_out, preferred_element_type=jnp.float32
        )
        d_prob = jnp.einsum("rhd,sd->hrs", grad_out, values, preferred_element_type=jnp.float32)
        d_score = (prob * (d_prob - delta[:, :, None])).astype(jnp.bfloat16)
        d_query = (
            jnp.einsum("hrs,sd->rhd", d_score, keys, preferred_element_type=jnp.float32) * scale
        )
        d_key = (
            jnp.einsum("hrs,rhd->sd", d_score, queries, preferred_element_type=jnp.float32) * scale
        )
        return (d_query, jnp.stack([d_key, d_value]))

    pair = jnp.stack([key_rows[0], value_rows[0]])
    query_zero = jnp.zeros((rows, heads, head_dim), jnp.float32)

    def pass_grads(sums):
        return passed_along(sums, "ctx", 1)

    def cycle_step(step, carry):
        pair_now, sums, query_sum = carry
        owner = (mine - step) % width
        d_query, d_kv = tile(pair_now, slot_positions(block_order, owner, half))
        sums = pass_grads(sums + d_kv)
        pair_now = passed_along(pair_now, "ctx", 1)
        return (pair_now, sums, query_sum + d_query)

    start = (pair, jnp.zeros((2, rows, head_dim), jnp.float32), query_zero)
    pair_last, sums, query_sum = lax.fori_loop(0, width - 1, cycle_step, start)
    d_query, d_kv = tile(pair_last, slot_positions(block_order, (mine + 1) % width, half))
    kv_sums = pass_grads(sums + d_kv)
    query_sum = query_sum + d_query
    d_query_out = query_sum.reshape(1, rows, heads * head_dim).astype(jnp.bfloat16)
    grads_bf = jnp.concatenate([kv_sums[0], kv_sums[1]], axis=1).astype(jnp.bfloat16)
    inputs = layer_input[0]
    d_weight = lax.psum_scatter(
        lax.dot_general(
            inputs, grads_bf, (((0,), (0,)), ((), ())), preferred_element_type=jnp.float32
        ),
        ("dp", "ctx"),
        scatter_dimension=0,
        tiled=True,
    )
    return (d_query_out, d_weight)


def solution(mesh):
    return jax.shard_map(
        body,
        mesh=mesh,
        in_specs=(
            P("dp", "ctx", None),
            P("dp", "ctx", None),
            P("dp", "ctx", None),
            P("dp", "ctx", None),
            P("dp", "ctx", None),
            P("dp", "ctx", None),
            P("dp", None, "ctx"),
            P(),
        ),
        out_specs=(P("dp", "ctx", None), P(("dp", "ctx"), None)),
        check_vma=False,
    )
```

profile of v0, /device:TPU:0, one launch (start us, length us, event | category | flops | bytes accessed | tf_op | source)
XLA Modules:
  0.0 217.5 jit_solution(2436954639523679326)
XLA Ops:
  7.2 1.3 copy.17
  8.5 0.3 copy.20
  8.8 0.2 copy.19
  9.1 1.3 copy.18
  10.4 0.3 copy.21
  10.7 0.2 fusion.27
  10.8 0.1 dynamic-slice_multiply_fusion.1
  10.9 0.1 add_bitcast_fusion.2
  11.0 0.7 broadcast_compare_fusion.1
  11.7 0.7 pad_maximum_fusion
  12.4 32.5 %while.20 = (s32[]{:T(128)}, bf16[2,256,128]{2,1,0:T(8,128)(2,1)}, f32[2,256,128]{2,1,0:T(8,128)S(1)}, f32[256,8,128]{2,0,1:T(8,128)S(1)}, s32[]{:T(128)}, /*ind...) while((s32[]{:T(128)}, bf16[2,256,128]{2,1,0:T(8,128)(2,1)}, ...), condition=%wide.region_2.3_spmd.clone, body=%wide.region_1.2_spmd.clone.sunk | while | flops 675774976 | bytes 16863680 | solution.py:68
  12.4 0.9 copy.44
  13.3 0.5 collective-permute-start
  13.8 0.1 dynamic-slice_multiply_fusion.4
  13.9 0.1 add_bitcast_fusion.7
  13.9 0.1 add_bitcast_fusion.6
  14.0 0.1 broadcast_compare_fusion.3
  14.1 1.3 fusion.75
  15.4 0.4 convolution_bitcast_fusion.6
  15.8 0.4 fusion.76
  16.3 0.4 fusion.77
  16.7 0.7 maximum_add_fusion.3
  17.5 2.6 %collective-permute-start.1 = (f32[2,256,128]{2,1,0:T(8,128)}, f32[2,256,128]{2,1,0:T(8,128)S(1)}, u32[]{:S(2)}, u32[]{:S(2)}) collective-permute-start(f32[2,256,128]{2,1,0:T(8,128)} %maximum_add_fusion.3), channel_id=1, source_target_pairs={{0,1},{1,2},{2,3},{3,0},{4,5},{5,6},{6,7},{7,4},{8,9},{9,10},{10,1... | collective-permute-start | bytes 786440 | tf_op jit(solution)/shard_map/while/body/eval_jaxpr/ppermute | solution.py:10
  20.1 0.9 fusion.78
  21.0 2.7 %collective-permute-done.1 = f32[2,256,128]{2,1,0:T(8,128)S(1)} collective-permute-done((f32[2,256,128]{2,1,0:T(8,128)}, f32[2,256,128]{2,1,0:T(8,128)S(1)}, u32[]{:S(2)}, u32[]{:S(2)}) %collective-permute-start.1) | collective-permute-done | bytes 262176 | tf_op jit(solution)/shard_map/while/body/eval_jaxpr/ppermute | solution.py:10
  23.7 0.9 copy.44
  24.6 0.0 collective-permute-start
  24.6 0.1 dynamic-slice_multiply_fusion.4
  24.7 0.1 add_bitcast_fusion.7
  24.8 0.1 add_bitcast_fusion.6
  24.8 0.1 broadcast_compare_fusion.3
  25.0 1.3 fusion.75
  26.2 0.4 convolution_bitcast_fusion.6
  26.7 0.4 fusion.76
  27.1 0.4 fusion.77
  27.6 0.7 maximum_add_fusion.3
  28.3 2.4 %collective-permute-start.1 = (f32[2,256,128]{2,1,0:T(8,128)}, f32[2,256,128]{2,1,0:T(8,128)S(1)}, u32[]{:S(2)}, u32[]{:S(2)}) collective-permute-start(f32[2,256,128]{2,1,0:T(8,128)} %maximum_add_fusion.3), channel_id=1, source_target_pairs={{0,1},{1,2},{2,3},{3,0},{4,5},{5,6},{6,7},{7,4},{8,9},{9,10},{10,1... | collective-permute-start | bytes 786440 | tf_op jit(solution)/shard_map/while/body/eval_jaxpr/ppermute | solution.py:10
  30.7 0.9 fusion.78
  31.6 2.7 %collective-permute-done.1 = f32[2,256,128]{2,1,0:T(8,128)S(1)} collective-permute-done((f32[2,256,128]{2,1,0:T(8,128)}, f32[2,256,128]{2,1,0:T(8,128)S(1)}, u32[]{:S(2)}, u32[]{:S(2)}) %collective-permute-start.1) | collective-permute-done | bytes 262176 | tf_op jit(solution)/shard_map/while/body/eval_jaxpr/ppermute | solution.py:10
  34.3 0.9 copy.44
  35.2 0.1 dynamic-slice_multiply_fusion.4
  35.3 0.1 add_bitcast_fusion.7
  35.4 0.1 add_bitcast_fusion.6
  35.5 0.1 broadcast_compare_fusion.3
  35.6 1.3 fusion.75
  36.9 0.4 convolution_bitcast_fusion.6
  37.3 0.4 fusion.76
  37.7 0.4 fusion.77
  38.2 0.7 maximum_add_fusion.3
  38.9 2.4 %collective-permute-start.1 = (f32[2,256,128]{2,1,0:T(8,128)}, f32[2,256,128]{2,1,0:T(8,128)S(1)}, u32[]{:S(2)}, u32[]{:S(2)}) collective-permute-start(f32[2,256,128]{2,1,0:T(8,128)} %maximum_add_fusion.3), channel_id=1, source_target_pairs={{0,1},{1,2},{2,3},{3,0},{4,5},{5,6},{6,7},{7,4},{8,9},{9,10},{10,1... | collective-permute-start | bytes 786440 | tf_op jit(solution)/shard_map/while/body/eval_jaxpr/ppermute | solution.py:10
  41.3 0.9 fusion.78
  42.2 2.7 %collective-permute-done.1 = f32[2,256,128]{2,1,0:T(8,128)S(1)} collective-permute-done((f32[2,256,128]{2,1,0:T(8,128)}, f32[2,256,128]{2,1,0:T(8,128)S(1)}, u32[]{:S(2)}, u32[]{:S(2)}) %collective-permute-start.1) | collective-permute-done | bytes 262176 | tf_op jit(solution)/shard_map/while/body/eval_jaxpr/ppermute | solution.py:10
  44.9 1.7 fusion.21
  46.6 0.4 convolution_bitcast_fusion.3
  47.1 1.4 fusion.19
  48.5 0.4 fusion.26
  49.0 0.1 collective-permute-start.2
  49.0 4.4 %collective-permute-done.2 = bf16[2,256,128]{2,1,0:T(8,128)(2,1)S(1)} collective-permute-done((bf16[2,256,128]{2,1,0:T(8,128)(2,1)S(1)}, bf16[2,256,128]{2,1,0:T(8,128)(2,1)S(1)}, u32[]{:S(2)}, u32[]{:S(2)}) %collective-permute-start.2) | collective-permute-done | bytes 131104 | tf_op jit(solution)/shard_map/ppermute | solution.py:10
  53.4 4.5 %convolution_bitcast_fusion.2 = f32[8192,256]{0,1:T(8,128)} fusion(bf16[1,256,8192]{2,1,0:T(8,128)(2,1)S(1)} %copy-done.4, bf16[256,128]{1,0:T(8,128)(2,1)S(1)} %get-tuple-element.349, bf16[256,128]{1,0:T(8,128)(2,1)S(1)} %get-tuple-element.348), kind=kOutput, calls=%fused_computation.26 | convolution fusion | flops 1074003968 | bytes 12713984 | tf_op jit(solution)/shard_map/dot_general | solution.py:76
  58.0 0.3 copy.26
  58.3 1.2 fusion.24
  59.5 1.0 copy.29
  60.5 148.4 %reduce-scatter.2.cloned.1.call-done = f32[256,256]{0,1:T(8,128)} async-done(((f32[8192,256]{0,1:T(8,128)}), f32[256,256]{0,1:T(8,128)}) %reduce-scatter.2.cloned.1.call-update) | async-done | bytes 262160 | tf_op jit(solution)/shard_map/reduce_scatter | solution.py:75
  208.9 1.8 copy.30
  (28 shorter events, 0.2 us)
Async XLA Ops:
  7.2 1.7 copy-start.5
  7.2 201.7 %reduce-scatter.2.cloned.1.call-start = ((), (), s32[]{:S(2)}) async-start(), calls=%async_computation.1 | async-start | bytes 8650752 | tf_op jit(solution)/shard_map/reduce_scatter | solution.py:75
  8.5 1.8 copy-start.2
  8.8 2.0 copy-start.8
  9.1 2.7 %copy-start.6 = (bf16[1,256,128]{2,1,0:T(8,128)(2,1)S(1)}, bf16[1,256,128]{2,1,0:T(8,128)(2,1)}, u32[]{:S(2)}) copy-start(bf16[1,256,128]{2,1,0:T(8,128)(2,1)} %param.13) | copy-start | bytes 196612
  9.1 2.7 %copy-start.7 = (bf16[1,256,128]{2,1,0:T(8,128)(2,1)S(1)}, bf16[1,256,128]{2,1,0:T(8,128)(2,1)}, u32[]{:S(2)}) copy-start(bf16[1,256,128]{2,1,0:T(8,128)(2,1)} %param.12) | copy-start | bytes 196612
  10.4 2.0 copy-start
  13.3 7.6 %collective-permute-start = (bf16[2,256,128]{2,1,0:T(8,128)(2,1)S(1)}, bf16[2,256,128]{2,1,0:T(8,128)(2,1)}, u32[]{:S(2)}, u32[]{:S(2)}) collective-permute-start(bf16[2,256,128]{2,1,0:T(8,128)(2,1)S(1)} %copy.44), channel_id=1, source_target_pairs={{0,1},{1,2},{2,3},{3,0},{4,5},{5,6},{6,7},{7,4},{8,9},{9,10},{10,1... | collective-permute-start | bytes 393224 | tf_op jit(solution)/shard_map/while/body/eval_jaxpr/ppermute | solution.py:10
  17.5 6.2 %collective-permute-start.1 = (f32[2,256,128]{2,1,0:T(8,128)}, f32[2,256,128]{2,1,0:T(8,128)S(1)}, u32[]{:S(2)}, u32[]{:S(2)}) collective-permute-start(f32[2,256,128]{2,1,0:T(8,128)} %maximum_add_fusion.3), channel_id=1, source_target_pairs={{0,1},{1,2},{2,3},{3,0},{4,5},{5,6},{6,7},{7,4},{8,9},{9,10},{10,1... | collective-permute-start | bytes 786440 | tf_op jit(solution)/shard_map/while/body/eval_jaxpr/ppermute | solution.py:10
  24.6 7.0 %collective-permute-start = (bf16[2,256,128]{2,1,0:T(8,128)(2,1)S(1)}, bf16[2,256,128]{2,1,0:T(8,128)(2,1)}, u32[]{:S(2)}, u32[]{:S(2)}) collective-permute-start(bf16[2,256,128]{2,1,0:T(8,128)(2,1)S(1)} %copy.44), channel_id=1, source_target_pairs={{0,1},{1,2},{2,3},{3,0},{4,5},{5,6},{6,7},{7,4},{8,9},{9,10},{10,1... | collective-permute-start | bytes 393224 | tf_op jit(solution)/shard_map/while/body/eval_jaxpr/ppermute | solution.py:10
  28.3 6.0 %collective-permute-start.1 = (f32[2,256,128]{2,1,0:T(8,128)}, f32[2,256,128]{2,1,0:T(8,128)S(1)}, u32[]{:S(2)}, u32[]{:S(2)}) collective-permute-start(f32[2,256,128]{2,1,0:T(8,128)} %maximum_add_fusion.3), channel_id=1, source_target_pairs={{0,1},{1,2},{2,3},{3,0},{4,5},{5,6},{6,7},{7,4},{8,9},{9,10},{10,1... | collective-permute-start | bytes 786440 | tf_op jit(solution)/shard_map/while/body/eval_jaxpr/ppermute | solution.py:10
  35.2 6.9 %collective-permute-start = (bf16[2,256,128]{2,1,0:T(8,128)(2,1)S(1)}, bf16[2,256,128]{2,1,0:T(8,128)(2,1)}, u32[]{:S(2)}, u32[]{:S(2)}) collective-permute-start(bf16[2,256,128]{2,1,0:T(8,128)(2,1)S(1)} %copy.44), channel_id=1, source_target_pairs={{0,1},{1,2},{2,3},{3,0},{4,5},{5,6},{6,7},{7,4},{8,9},{9,10},{10,1... | collective-permute-start | bytes 393224 | tf_op jit(solution)/shard_map/while/body/eval_jaxpr/ppermute | solution.py:10
  38.9 6.0 %collective-permute-start.1 = (f32[2,256,128]{2,1,0:T(8,128)}, f32[2,256,128]{2,1,0:T(8,128)S(1)}, u32[]{:S(2)}, u32[]{:S(2)}) collective-permute-start(f32[2,256,128]{2,1,0:T(8,128)} %maximum_add_fusion.3), channel_id=1, source_target_pairs={{0,1},{1,2},{2,3},{3,0},{4,5},{5,6},{6,7},{7,4},{8,9},{9,10},{10,1... | collective-permute-start | bytes 786440 | tf_op jit(solution)/shard_map/while/body/eval_jaxpr/ppermute | solution.py:10
  44.9 1.7 copy-start.1
  47.1 1.4 copy-start.3
  47.1 6.4 %copy-start.4 = (bf16[1,256,8192]{2,1,0:T(8,128)(2,1)S(1)}, bf16[1,256,8192]{2,1,0:T(8,128)(2,1)}, u32[]{:S(2)}) copy-start(bf16[1,256,8192]{2,1,0:T(8,128)(2,1)} %param.10) | copy-start | bytes 12582916
  49.0 4.4 %collective-permute-start.2 = (bf16[2,256,128]{2,1,0:T(8,128)(2,1)S(1)}, bf16[2,256,128]{2,1,0:T(8,128)(2,1)S(1)}, u32[]{:S(2)}, u32[]{:S(2)}) collective-permute-start(bf16[2,256,128]{2,1,0:T(8,128)(2,1)S(1)} %maximum_add_fusion.1), channel_id=1, source_target_pairs={{0,1},{1,2},{2,3},{3,0},{4,5},{5,6},{6,7},{7,4},{8,9},{9,10},{10,1... | collective-permute-start | bytes 393224 | tf_op jit(solution)/shard_map/ppermute | solution.py:10
Sparse Core Ops, SparseCore 0:
  58.1 150.7 reduce-scatter.1
where the time goes:
time: 218 us
  waiting for transfers between devices  161 us (74%)
  matrix products  20 us (9%)
  between operations  14.3 us (7%)
  local copies, waits for them, and re-layouts  9.23 us (4%)
  starting transfers between devices  7.94 us (4%)
  other arithmetic  4.94 us (2%)
    reduce_scatter x1, waiting for transfers between devices, body(): lax.psum_scatter(lax.dot_general(inputs, grads_bf, (((0,), (0,)), ((), ()...  148 us
    ppermute x7, waiting for transfers between devices, passed_along(): return lax.ppermute(value, axis, pairs)  12.6 us
    ppermute x7, starting transfers between devices, passed_along(): return lax.ppermute(value, axis, pairs)  7.9 us
    unnamed x25, local copies, waits for them, and re-layouts  6.15 us
    dot_general x4, matrix products, tile(): jnp.einsum('rhd,sd->hrs', queries, keys, preferred_element_type=jnp.float32)  5.5 us
    dot_general x1, matrix products, body(): lax.dot_general(inputs, grads_bf, (((0,), (0,)), ((), ())), preferred_ele...  4.51 us
  transfers between devices with their start and end apart: 8, of which 5 were waited for; matrix products, arithmetic and copies ran while one was open for 7% of the time, Pallas kernels for 0%

commit v1 on v0

--- a/solution.py
+++ b/solution.py
@@ -1,7 +1,15 @@
 import jax
 import jax.numpy as jnp
 from jax import lax
+from jax.experimental import pallas as pl
+from jax.experimental.pallas import tpu as pltpu
 from jax.sharding import PartitionSpec as P
+
+MESH = pl.DeviceIdType.MESH
+F32 = jnp.float32
+BF16 = jnp.bfloat16
+LOG2E = 1.4426950408889634
+STRIPS = (2, 1, 3, 0)
 
 
 def passed_along(value, axis, steps):
@@ -83,9 +91,307 @@
     return (d_query_out, d_weight)
 
 
+def dot(left, right, contract=((1,), (0,))):
+    return lax.dot_general(left, right, (contract, ((), ())), preferred_element_type=F32)
+
+
+def fused_kernel(
+    x_ref, q_ref, k_ref, v_ref, o_ref, do_ref, lse_ref, order_ref,
+    dq_ref, dw_ref,
+    xbuf, kv, lse2, delta, dq_acc, own, acc, g_send, g_recv, g_mine, g_other,
+    a_keep, b_keep, a1_send, a1_recv, b1_send, b1_recv,
+    a2_send, a2_recv, b2_send, b2_recv, last_keep, last_send, last_recv,
+    x_local, x_send, x_recv, kv_ssem, kv_rsem, g_ssem, g_rsem,
+    a1_ssem, a1_rsem, b1_ssem, b1_rsem, a2_ssem, a2_rsem, b2_ssem, b2_rsem,
+    last_ssem, last_rsem,
+):
+    rows, dh = k_ref.shape[1], k_ref.shape[2]
+    heads = q_ref.shape[2] // dh
+    half = rows // 2
+    scale = dh ** (-0.5)
+    dp, ctx = lax.axis_index("dp"), lax.axis_index("ctx")
+    z, y = dp // 2, dp % 2
+    x, c = ctx // 2, ctx % 2
+    mate = (dp, 2 * x + 1 - c)
+    side = (dp, 2 * (1 - x) + c)
+    cross = (dp, 2 * (1 - x) + 1 - c)
+    over = (2 * z + 1 - y, ctx)
+    along = [(2 * ((z + k) % 4) + y, ctx) for k in (1, 2, 3)]
+
+    barrier = pltpu.get_barrier_semaphore()
+    everyone = [mate, side, cross, over] + along
+    for peer in everyone:
+        pl.semaphore_signal(barrier, inc=1, device_id=peer, device_id_type=MESH)
+    kv[0, :, 0:dh] = k_ref[0]
+    kv[0, :, dh : 2 * dh] = v_ref[0]
+    pl.semaphore_wait(barrier, len(everyone))
+
+    started = []
+
+    def send(source, target, ssem, rsem, peer):
+        copy = pltpu.make_async_remote_copy(
+            src_ref=source, dst_ref=target, send_sem=ssem, recv_sem=rsem,
+            device_id=peer, device_id_type=MESH,
+        )
+        copy.start()
+        started.append(copy)
+        return copy
+
+    kv_side = send(kv.at[0], kv.at[1], kv_ssem.at[0], kv_rsem.at[0], side)
+    kv_mate = send(kv.at[0], kv.at[3], kv_ssem.at[2], kv_rsem.at[2], mate)
+
+    def x_copies(m):
+        mine = pl.ds(pl.multiple_of((2 * m + c) * rows, rows), rows)
+        theirs = pl.ds(pl.multiple_of((2 * m + 1 - c) * rows, rows), rows)
+        here = pltpu.make_async_copy(
+            x_ref.at[0, :, mine], xbuf.at[m, pl.ds(0, rows), :], x_local.at[m]
+        )
+        there = pltpu.make_async_remote_copy(
+            src_ref=x_ref.at[0, :, theirs], dst_ref=xbuf.at[m, pl.ds(rows, rows), :],
+            send_sem=x_send.at[m], recv_sem=x_recv.at[m], device_id=mate, device_id_type=MESH,
+        )
+        return here, there
+
+    @pl.loop(0, 16)
+    def _(m):
+        here, there = x_copies(m)
+        there.start()
+        here.start()
+
+    lse2[...] = lse_ref[0] * LOG2E
+
+    @pl.loop(0, heads)
+    def _(h):
+        cols = pl.ds(pl.multiple_of(h * dh, dh), dh)
+        product = do_ref[0, :, cols].astype(F32) * o_ref[0, :, cols].astype(F32)
+        delta[pl.ds(h, 1), :] = jnp.sum(product.T, axis=0, keepdims=True)
+
+    ahead = lax.broadcasted_iota(jnp.int32, (half, half), 1) - lax.broadcasted_iota(
+        jnp.int32, (half, half), 0
+    )
+
+    def chunk(slot, owner, total, first):
+        keys = kv[slot, :, 0:dh]
+        values = kv[slot, :, dh : 2 * dh]
+        keys_t = keys.astype(F32).T.astype(BF16)
+        total[...] = jnp.zeros_like(total)
+
+        def visible():
+            return jnp.concatenate(
+                [
+                    jnp.concatenate(
+                        [
+                            ahead >= (order_ref[2 * owner + a] - order_ref[2 * ctx + b]) * half
+                            for b in range(2)
+                        ],
+                        axis=1,
+                    )
+                    for a in range(2)
+                ],
+                axis=0,
+            )
+
+        def one(h):
+            cols = pl.ds(pl.multiple_of(h * dh, dh), dh)
+            query = q_ref[0, :, cols]
+            grad = do_ref[0, :, cols]
+            score = dot(keys, query, ((1,), (1,)))
+            d_prob = dot(values, grad, ((1,), (1,)))
+            prob = jnp.where(
+                visible(), jnp.exp2(score * (scale * LOG2E) - lse2[pl.ds(h, 1), :]), 0.0
+            )
+            prob_b = prob.astype(BF16)
+            d_score = (prob * (d_prob - delta[pl.ds(h, 1), :])).astype(BF16)
+            d_value = dot(prob_b, grad)
+            d_key = dot(d_score, query)
+            d_query = dot(keys_t, d_score)
+            if first:
+                dq_acc[h] = d_query
+            else:
+                dq_acc[h] += d_query
+            return d_key, d_value
+
+        @pl.loop(0, heads // 2)
+        def _(pair):
+            key_a, value_a = one(2 * pair)
+            key_b, value_b = one(2 * pair + 1)
+            total[:, 0:dh] += key_a + key_b
+            total[:, dh : 2 * dh] += value_a + value_b
+
+    def give(slot, peer):
+        g_send[slot - 1, :, 0:dh] = (acc[:, 0:dh] * scale).astype(BF16)
+        g_send[slot - 1, :, dh : 2 * dh] = acc[:, dh : 2 * dh].astype(BF16)
+        return send(
+            g_send.at[slot - 1], g_recv.at[slot - 1], g_ssem.at[slot - 1], g_rsem.at[slot - 1], peer
+        )
+
+    chunk(0, ctx, own, True)
+    kv_side.wait_recv()
+    kv_cross = send(kv.at[1], kv.at[2], kv_ssem.at[1], kv_rsem.at[1], mate)
+    chunk(1, side[1], acc, False)
+    given = [give(1, side)]
+    kv_cross.wait_recv()
+    chunk(2, cross[1], acc, False)
+    given.append(give(2, cross))
+    kv_mate.wait_recv()
+    chunk(3, mate[1], acc, False)
+    given.append(give(3, mate))
+
+    @pl.loop(0, heads)
+    def _(h):
+        cols = pl.ds(pl.multiple_of(h * dh, dh), dh)
+        dq_ref[0, :, cols] = (dq_acc[h] * scale).T.astype(BF16)
+
+    for copy in given:
+        copy.wait_recv()
+    d_key = own[:, 0:dh] * scale
+    d_value = own[:, dh : 2 * dh]
+    for slot in range(3):
+        d_key = d_key + g_recv[slot, :, 0:dh].astype(F32)
+        d_value = d_value + g_recv[slot, :, dh : 2 * dh].astype(F32)
+    g_mine[0:dh, :] = d_key.T.astype(BF16)
+    g_mine[dh : 2 * dh, :] = d_value.T.astype(BF16)
+    g_copy = send(g_mine, g_other, g_ssem.at[3], g_rsem.at[3], mate)
+
+    @pl.loop(0, 16)
+    def _(m):
+        here, there = x_copies(m)
+        here.wait()
+        there.wait()
+
+    g_copy.wait_recv()
+
+    first_a, first_b, second_a, second_b, final = {}, {}, {}, {}, {}
+
+    def stage_one(k):
+        strip = (z + k) % 4
+        for yr in range(2):
+            for xr in range(2):
+                m = strip * 4 + (y + yr) % 2 * 2 + (x + xr) % 2
+                part = dot(g_mine[...], xbuf[m, 0:rows, :]) + dot(
+                    g_other[...], xbuf[m, rows : 2 * rows, :]
+                )
+                if xr:
+                    a1_send[k, yr] = part[0:dh].astype(BF16)
+                else:
+                    a_keep[k, yr] = part[0:dh]
+                if yr:
+                    b1_send[k, xr] = part[dh : 2 * dh].astype(BF16)
+                else:
+                    b_keep[k, xr] = part[dh : 2 * dh]
+        first_a[k] = send(a1_send.at[k], a1_recv.at[k], a1_ssem.at[k], a1_rsem.at[k], side)
+        first_b[k] = send(b1_send.at[k], b1_recv.at[k], b1_ssem.at[k], b1_rsem.at[k], over)
+
+    def stage_two(k):
+        first_a[k].wait_recv()
+        a2_send[k] = (a_keep[k, 1] + a1_recv[k, 1].astype(F32)).astype(BF16)
+        second_a[k] = send(a2_send.at[k], a2_recv.at[k], a2_ssem.at[k], a2_rsem.at[k], over)
+        first_b[k].wait_recv()
+        b2_send[k] = (b_keep[k, 1] + b1_recv[k, 1].astype(F32)).astype(BF16)
+        second_b[k] = send(b2_send.at[k], b2_recv.at[k], b2_ssem.at[k], b2_rsem.at[k], side)
+
+    def stage_three(k):
+        second_a[k].wait_recv()
+        second_b[k].wait_recv()
+        sum_a = a_keep[k, 0] + a1_recv[k, 0].astype(F32) + a2_recv[k].astype(F32)
+        sum_b = b_keep[k, 0] + b1_recv[k, 0].astype(F32) + b2_recv[k].astype(F32)
+        if k:
+            last_send[k - 1, 0:dh, :] = sum_a.astype(BF16)
+            last_send[k - 1, dh : 2 * dh, :] = sum_b.astype(BF16)
+            final[k] = send(
+                last_send.at[k - 1], last_recv.at[k - 1],
+                last_ssem.at[k - 1], last_rsem.at[k - 1], along[k - 1],
+            )
+        else:
+            last_keep[0:dh, :] = sum_a
+            last_keep[dh : 2 * dh, :] = sum_b
+
+    s = STRIPS
+    stage_one(s[0])
+    stage_one(s[1])
+    stage_two(s[0])
+    stage_one(s[2])
+    stage_two(s[1])
+    stage_three(s[0])
+    stage_one(s[3])
+    stage_two(s[2])
+    stage_three(s[1])
+    stage_two(s[3])
+    stage_three(s[2])
+    stage_three(s[3])
+    for k in (1, 2, 3):
+        final[k].wait_recv()
+    result = last_keep[...]
+    for k in range(3):
+        result = result + last_recv[k].astype(F32)
+    dw_ref[...] = result.T
+    for copy in started:
+        copy.wait_send()
+
+
+def fused_body(layer_input, query_rows, key_rows, value_rows, attn_out, d_attn, log_sum_exp, block_order):
+    rows, dh = key_rows.shape[1], key_rows.shape[2]
+    heads = query_rows.shape[2] // dh
+    wide = 2 * dh
+    vmem = pl.BlockSpec(memory_space=pltpu.VMEM)
+    dma = pltpu.SemaphoreType.DMA
+    return pl.pallas_call(
+        fused_kernel,
+        out_shape=(
+            jax.ShapeDtypeStruct(query_rows.shape, BF16),
+            jax.ShapeDtypeStruct((rows, wide), F32),
+        ),
+        in_specs=[pl.BlockSpec(memory_space=pl.ANY)] + [vmem] * 6 + [pl.BlockSpec(memory_space=pltpu.SMEM)],
+        out_specs=(vmem, vmem),
+        scratch_shapes=[
+            pltpu.VMEM((16, 2 * rows, rows), BF16),
+            pltpu.VMEM((4, rows, wide), BF16),
+            pltpu.VMEM((heads, rows), F32),
+            pltpu.VMEM((heads, rows), F32),
+            pltpu.VMEM((heads, dh, rows), F32),
+            pltpu.VMEM((rows, wide), F32),
+            pltpu.VMEM((rows, wide), F32),
+            pltpu.VMEM((3, rows, wide), BF16),
+            pltpu.VMEM((3, rows, wide), BF16),
+            pltpu.VMEM((wide, rows), BF16),
+            pltpu.VMEM((wide, rows), BF16),
+            pltpu.VMEM((4, 2, dh, rows), F32),
+            pltpu.VMEM((4, 2, dh, rows), F32),
+            pltpu.VMEM((4, 2, dh, rows), BF16),
+            pltpu.VMEM((4, 2, dh, rows), BF16),
+            pltpu.VMEM((4, 2, dh, rows), BF16),
+            pltpu.VMEM((4, 2, dh, rows), BF16),
+            pltpu.VMEM((4, dh, rows), BF16),
+            pltpu.VMEM((4, dh, rows), BF16),
+            pltpu.VMEM((4, dh, rows), BF16),
+            pltpu.VMEM((4, dh, rows), BF16),
+            pltpu.VMEM((wide, rows), F32),
+            pltpu.VMEM((3, wide, rows), BF16),
+            pltpu.VMEM((3, wide, rows), BF16),
+            dma((16,)), dma((16,)), dma((16,)),
+            dma((3,)), dma((3,)), dma((4,)), dma((4,)),
+            dma((4,)), dma((4,)), dma((4,)), dma((4,)),
+            dma((4,)), dma((4,)), dma((4,)), dma((4,)),
+            dma((3,)), dma((3,)),
+        ],
+        compiler_params=pltpu.CompilerParams(
+            collective_id=0, has_side_effects=True, vmem_limit_bytes=40 * 1024 * 1024
+        ),
+        cost_estimate=pl.CostEstimate(
+            flops=4 * 10 * heads * rows * rows * dh + 4 * rows * rows * wide * 16,
+            bytes_accessed=8 * 1024 * 1024,
+            transcendentals=4 * heads * rows * rows,
+        ),
+    )(layer_input, query_rows, key_rows, value_rows, attn_out, d_attn, log_sum_exp, block_order)
+
+
+def fits(mesh):
+    return dict(mesh.shape) == {"dp": 8, "ctx": 4}
+
+
 def solution(mesh):
     return jax.shard_map(
-        body,
+        fused_body if fits(mesh) else body,
         mesh=mesh,
         in_specs=(
             P("dp", "ctx", None),

time: 218 us -> 55.4 us (0.25)
  waiting for transfers between devices: 161 us -> 0 us
  Pallas kernels: 0 us -> 44.5 us
  matrix products: 20 us -> 0 us
  between operations: 14.3 us -> 0.66 us
  starting transfers between devices: 7.94 us -> 0 us
  other arithmetic: 4.94 us -> 0 us
    reduce_scatter x1 -> x0, waiting for transfers between devices: 148 us -> none  [body(): lax.psum_scatter(lax.dot_general(inputs, grads_bf, (((0,), (0,)), ((), ()...]
    pallas_call x0 -> x1, Pallas kernels: none -> 44.5 us  [fused_body(): pl.pallas_call(fused_kernel, out_shape=(jax.ShapeDtypeStruct(query_rows.s...]
    dot_general x21 -> x0, matrix products: 20 us -> none  [the longest x4 5.5 us: tile(): jnp.einsum('rhd,sd->hrs', queries, keys, preferred_element_type=jnp.float32)]
    ppermute x7 -> x0, waiting for transfers between devices: 12.6 us -> none  [passed_along(): return lax.ppermute(value, axis, pairs)]
    ppermute x7 -> x0, starting transfers between devices: 7.9 us -> none  [passed_along(): return lax.ppermute(value, axis, pairs)]
    unnamed x25 -> x18, local copies, waits for them, and re-layouts: 6.15 us -> 9.83 us
    while x4 -> x0, local copies, waits for them, and re-layouts: 3.05 us -> none
    add x8 -> x0, other arithmetic: 2.56 us -> none  [the longest x3 2.24 us: cycle_step(): sums = pass_grads(sums + d_kv)]
  transfers between devices with their start and end apart: 8 -> 0, of which waited for: 5 -> 0; matrix products, arithmetic and copies ran while one was open for 7% -> 0% of each run, Pallas kernels for 0% -> 0%
where the time goes in v1:
time: 55.4 us; the launch traced here: 55 us
  Pallas kernels  44.5 us (80%)
  local copies, waits for them, and re-layouts  9.83 us (18%)
  between operations  0.66 us (1%)
    pallas_call x1, Pallas kernels, fused_body(): pl.pallas_call(fused_kernel, out_shape=(jax.ShapeDtypeStruct(query_rows.s...  44.5 us
    unnamed x18, local copies, waits for them, and re-layouts  9.83 us

profile of v1, /device:TPU:0, one launch (start us, length us, event | category | flops | bytes accessed | tf_op | source)
XLA Modules:
  0.0 55.0 jit_solution(11931715663042211059)
XLA Ops:
  0.6 0.0 copy-start
  0.6 2.2 %copy-done = bf16[1,256,8192]{2,1,0:T(8,128)(2,1)S(1)} copy-done((bf16[1,256,8192]{2,1,0:T(8,128)(2,1)S(1)}, bf16[1,256,8192]{2,1,0:T(8,128)(2,1)}, u32[]{:S(2)}) %copy-start) | copy-done | bytes 4194328
  2.8 0.0 copy-start.1
  2.8 1.0 %copy-done.1 = bf16[1,256,1024]{2,1,0:T(8,128)(2,1)S(1)} copy-done((bf16[1,256,1024]{2,1,0:T(8,128)(2,1)S(1)}, bf16[1,256,1024]{2,1,0:T(8,128)(2,1)}, u32[]{:S(2)}) %copy-start.1) | copy-done | bytes 524312
  3.9 0.0 copy-start.2
  3.9 1.0 %copy-done.2 = bf16[1,256,1024]{2,1,0:T(8,128)(2,1)S(1)} copy-done((bf16[1,256,1024]{2,1,0:T(8,128)(2,1)S(1)}, bf16[1,256,1024]{2,1,0:T(8,128)(2,1)}, u32[]{:S(2)}) %copy-start.2) | copy-done | bytes 524312
  4.9 0.0 copy-start.3
  4.9 1.0 %copy-done.3 = bf16[1,256,1024]{2,1,0:T(8,128)(2,1)S(1)} copy-done((bf16[1,256,1024]{2,1,0:T(8,128)(2,1)S(1)}, bf16[1,256,1024]{2,1,0:T(8,128)(2,1)}, u32[]{:S(2)}) %copy-start.3) | copy-done | bytes 524312
  5.9 0.0 copy-start.4
  6.0 0.8 %copy-done.4 = bf16[1,256,128]{2,1,0:T(8,128)(2,1)S(1)} copy-done((bf16[1,256,128]{2,1,0:T(8,128)(2,1)S(1)}, bf16[1,256,128]{2,1,0:T(8,128)(2,1)}, u32[]{:S(2)}) %copy-start.4) | copy-done | bytes 65560
  6.8 0.0 copy-start.5
  6.8 0.8 %copy-done.5 = bf16[1,256,128]{2,1,0:T(8,128)(2,1)S(1)} copy-done((bf16[1,256,128]{2,1,0:T(8,128)(2,1)S(1)}, bf16[1,256,128]{2,1,0:T(8,128)(2,1)}, u32[]{:S(2)}) %copy-start.5) | copy-done | bytes 65560
  7.6 0.0 copy-start.6
  7.6 0.7 %copy-done.6 = f32[1,8,256]{2,1,0:T(8,128)S(1)} copy-done((f32[1,8,256]{2,1,0:T(8,128)S(1)}, f32[1,8,256]{2,1,0:T(8,128)}, u32[]{:S(2)}) %copy-start.6) | copy-done | bytes 8216
  8.3 0.0 copy-start.7
  8.3 0.7 %copy-done.7 = s32[8]{0:T(128)S(1)} copy-done((s32[8]{0:T(128)S(1)}, s32[8]{0:T(128)}, u32[]{:S(2)}) %copy-start.7) | copy-done | bytes 56
  9.0 44.5 %shard_map.95 = (bf16[1,256,1024]{2,1,0:T(8,128)(2,1)S(1)}, f32[256,256]{1,0:T(8,128)S(1)}) custom-call(bf16[1,256,8192]{2,1,0:T(8,128)(2,1)S(1)} %copy-done, bf16[1,256,1024]{2,1,0:T(8,128)(2,1)S(1)} %copy-done.1, bf16[1,256,128]{2,1,0:T(8,128)(2,1)S(1)} %copy-done.4, bf16[1,256,128]{2,1,0:T(8,128)(2,1)S(1)} %copy-done.5, ...), custom_call_target="tpu_custom_call" | custom-call | flops 3758096384 | bytes 8388608 | tf_op jit(solution)/shard_map/pallas_call | solution.py:338
  53.5 0.8 %copy.12 = bf16[1,256,1024]{2,1,0:T(8,128)(2,1)} copy(bf16[1,256,1024]{2,1,0:T(8,128)(2,1)S(1)} %get-tuple-element.4) | data formatting | bytes 1048576
  54.3 0.7 %copy.13 = f32[256,256]{1,0:T(8,128)} copy(f32[256,256]{1,0:T(8,128)S(1)} %get-tuple-element.5) | data formatting | bytes 524288
Async XLA Ops:
  0.6 2.2 %copy-start = (bf16[1,256,8192]{2,1,0:T(8,128)(2,1)S(1)}, bf16[1,256,8192]{2,1,0:T(8,128)(2,1)}, u32[]{:S(2)}) copy-start(bf16[1,256,8192]{2,1,0:T(8,128)(2,1)} %x_ref.1) | copy-start | bytes 12582916
  2.8 1.0 %copy-start.1 = (bf16[1,256,1024]{2,1,0:T(8,128)(2,1)S(1)}, bf16[1,256,1024]{2,1,0:T(8,128)(2,1)}, u32[]{:S(2)}) copy-start(bf16[1,256,1024]{2,1,0:T(8,128)(2,1)} %q_ref.1) | copy-start | bytes 1572868
  3.9 1.0 %copy-start.2 = (bf16[1,256,1024]{2,1,0:T(8,128)(2,1)S(1)}, bf16[1,256,1024]{2,1,0:T(8,128)(2,1)}, u32[]{:S(2)}) copy-start(bf16[1,256,1024]{2,1,0:T(8,128)(2,1)} %o_ref.1) | copy-start | bytes 1572868
  4.9 1.0 %copy-start.3 = (bf16[1,256,1024]{2,1,0:T(8,128)(2,1)S(1)}, bf16[1,256,1024]{2,1,0:T(8,128)(2,1)}, u32[]{:S(2)}) copy-start(bf16[1,256,1024]{2,1,0:T(8,128)(2,1)} %do_ref.1) | copy-start | bytes 1572868
  5.9 0.8 %copy-start.4 = (bf16[1,256,128]{2,1,0:T(8,128)(2,1)S(1)}, bf16[1,256,128]{2,1,0:T(8,128)(2,1)}, u32[]{:S(2)}) copy-start(bf16[1,256,128]{2,1,0:T(8,128)(2,1)} %k_ref.1) | copy-start | bytes 196612
  6.8 0.8 %copy-start.5 = (bf16[1,256,128]{2,1,0:T(8,128)(2,1)S(1)}, bf16[1,256,128]{2,1,0:T(8,128)(2,1)}, u32[]{:S(2)}) copy-start(bf16[1,256,128]{2,1,0:T(8,128)(2,1)} %v_ref.1) | copy-start | bytes 196612
  7.6 0.7 %copy-start.6 = (f32[1,8,256]{2,1,0:T(8,128)S(1)}, f32[1,8,256]{2,1,0:T(8,128)}, u32[]{:S(2)}) copy-start(f32[1,8,256]{2,1,0:T(8,128)} %lse_ref.1) | copy-start | bytes 24580
  8.3 0.7 %copy-start.7 = (s32[8]{0:T(128)S(1)}, s32[8]{0:T(128)}, u32[]{:S(2)}) copy-start(s32[8]{0:T(128)} %order_ref.1) | copy-start | bytes 100

commit v2 on v1

--- a/solution.py
+++ b/solution.py
@@ -96,16 +96,16 @@
 
 
 def fused_kernel(
-    x_ref, q_ref, k_ref, v_ref, o_ref, do_ref, lse_ref, order_ref,
+    x_ref, q_hbm, k_hbm, v_hbm, o_hbm, do_hbm, lse_hbm, order_ref,
     dq_ref, dw_ref,
-    xbuf, kv, lse2, delta, dq_acc, own, acc, g_send, g_recv, g_mine, g_other,
+    q_ref, o_ref, do_ref, lse_ref, xbuf, kv, lse2, delta, dq_acc, own, acc, g_send, g_recv, g_mine, g_other,
     a_keep, b_keep, a1_send, a1_recv, b1_send, b1_recv,
     a2_send, a2_recv, b2_send, b2_recv, last_keep, last_send, last_recv,
     x_local, x_send, x_recv, kv_ssem, kv_rsem, g_ssem, g_rsem,
     a1_ssem, a1_rsem, b1_ssem, b1_rsem, a2_ssem, a2_rsem, b2_ssem, b2_rsem,
-    last_ssem, last_rsem,
+    last_ssem, last_rsem, in_sem,
 ):
-    rows, dh = k_ref.shape[1], k_ref.shape[2]
+    rows, dh = k_hbm.shape[1], k_hbm.shape[2]
     heads = q_ref.shape[2] // dh
     half = rows // 2
     scale = dh ** (-0.5)
@@ -118,13 +118,29 @@
     over = (2 * z + 1 - y, ctx)
     along = [(2 * ((z + k) % 4) + y, ctx) for k in (1, 2, 3)]
 
+    loads = [
+        pltpu.make_async_copy(source, target, in_sem.at[i])
+        for i, (source, target) in enumerate(
+            (
+                (k_hbm.at[0], kv.at[0, :, pl.ds(0, dh)]),
+                (v_hbm.at[0], kv.at[0, :, pl.ds(dh, dh)]),
+                (do_hbm, do_ref),
+                (o_hbm, o_ref),
+                (q_hbm, q_ref),
+                (lse_hbm, lse_ref),
+            )
+        )
+    ]
+    for copy in loads:
+        copy.start()
+
     barrier = pltpu.get_barrier_semaphore()
     everyone = [mate, side, cross, over] + along
     for peer in everyone:
         pl.semaphore_signal(barrier, inc=1, device_id=peer, device_id_type=MESH)
-    kv[0, :, 0:dh] = k_ref[0]
-    kv[0, :, dh : 2 * dh] = v_ref[0]
     pl.semaphore_wait(barrier, len(everyone))
+    loads[0].wait()
+    loads[1].wait()
 
     started = []
 
@@ -158,6 +174,8 @@
         there.start()
         here.start()
 
+    for copy in loads[2:]:
+        copy.wait()
     lse2[...] = lse_ref[0] * LOG2E
 
     @pl.loop(0, heads)
@@ -211,12 +229,11 @@
                 dq_acc[h] += d_query
             return d_key, d_value
 
-        @pl.loop(0, heads // 2)
-        def _(pair):
-            key_a, value_a = one(2 * pair)
-            key_b, value_b = one(2 * pair + 1)
-            total[:, 0:dh] += key_a + key_b
-            total[:, dh : 2 * dh] += value_a + value_b
+        @pl.loop(0, heads // 4)
+        def _(group):
+            parts = [one(4 * group + i) for i in range(4)]
+            total[:, 0:dh] += (parts[0][0] + parts[1][0]) + (parts[2][0] + parts[3][0])
+            total[:, dh : 2 * dh] += (parts[0][1] + parts[1][1]) + (parts[2][1] + parts[3][1])
 
     def give(slot, peer):
         g_send[slot - 1, :, 0:dh] = (acc[:, 0:dh] * scale).astype(BF16)
@@ -341,9 +358,13 @@
             jax.ShapeDtypeStruct(query_rows.shape, BF16),
             jax.ShapeDtypeStruct((rows, wide), F32),
         ),
-        in_specs=[pl.BlockSpec(memory_space=pl.ANY)] + [vmem] * 6 + [pl.BlockSpec(memory_space=pltpu.SMEM)],
+        in_specs=[pl.BlockSpec(memory_space=pltpu.HBM)] * 7 + [pl.BlockSpec(memory_space=pltpu.SMEM)],
         out_specs=(vmem, vmem),
         scratch_shapes=[
+            pltpu.VMEM(query_rows.shape, BF16),
+            pltpu.VMEM(query_rows.shape, BF16),
+            pltpu.VMEM(query_rows.shape, BF16),
+            pltpu.VMEM(log_sum_exp.shape, F32),
             pltpu.VMEM((16, 2 * rows, rows), BF16),
             pltpu.VMEM((4, rows, wide), BF16),
             pltpu.VMEM((heads, rows), F32),
@@ -372,10 +393,10 @@
             dma((3,)), dma((3,)), dma((4,)), dma((4,)),
             dma((4,)), dma((4,)), dma((4,)), dma((4,)),
             dma((4,)), dma((4,)), dma((4,)), dma((4,)),
-            dma((3,)), dma((3,)),
+            dma((3,)), dma((3,)), dma((6,)),
         ],
         compiler_params=pltpu.CompilerParams(
-            collective_id=0, has_side_effects=True, vmem_limit_bytes=40 * 1024 * 1024
+            collective_id=0, has_side_effects=True, vmem_limit_bytes=64 * 1024 * 1024
         ),
         cost_estimate=pl.CostEstimate(
             flops=4 * 10 * heads * rows * rows * dh + 4 * rows * rows * wide * 16,

time: 55.4 us -> 49.5 us (0.89)
  local copies, waits for them, and re-layouts: 9.83 us -> 3.54 us
  Pallas kernels: 44.5 us -> 45.1 us
    unnamed x18 -> x2, local copies, waits for them, and re-layouts: 9.83 us -> 3.54 us
    pallas_call x1, Pallas kernels: 44.5 us -> 45.1 us  [fused_body(): pl.pallas_call(fused_kernel, out_shape=(jax.ShapeDtypeStruct(query_rows.s...]
where the time goes in v2:
time: 49.5 us; the launch traced here: 49.3 us
  Pallas kernels  45.1 us (91%)
  local copies, waits for them, and re-layouts  3.54 us (7%)
  between operations  0.64 us (1%)
    pallas_call x1, Pallas kernels, fused_body(): pl.pallas_call(fused_kernel, out_shape=(jax.ShapeDtypeStruct(query_rows.s...  45.1 us
    unnamed x2, local copies, waits for them, and re-layouts  3.54 us

profile of v2, /device:TPU:0, one launch (start us, length us, event | category | flops | bytes accessed | tf_op | source)
XLA Modules:
  0.0 49.3 jit_solution(11172821670318410005)
XLA Ops:
  0.6 45.1 %shard_map.95 = (bf16[1,256,1024]{2,1,0:T(8,128)(2,1)}, f32[256,256]{1,0:T(8,128)}) custom-call(bf16[1,256,8192]{2,1,0:T(8,128)(2,1)} %x_ref.1, bf16[1,256,1024]{2,1,0:T(8,128)(2,1)} %q_hbm.1, bf16[1,256,128]{2,1,0:T(8,128)(2,1)} %k_hbm.1, bf16[1,256,128]{2,1,0:T(8,128)(2,1)} %v_hbm.1, bf16[1,256,1024]{2,1,0:T(8,128)(2,1)} %o_hbm.1, ...), custom_call_target="tpu_custom_call" | custom-call | flops 3758096384 | bytes 8388608 | tf_op jit(solution)/shard_map/pallas_call | solution.py:355
  45.7 1.9 %copy.12 = bf16[1,256,1024]{2,1,0:T(8,128)(2,1)} copy(bf16[1,256,1024]{2,1,0:T(8,128)(2,1)} %get-tuple-element.4) | data formatting | bytes 1048576
  47.6 1.7 %copy.13 = f32[256,256]{1,0:T(8,128)} copy(f32[256,256]{1,0:T(8,128)} %get-tuple-element.5) | data formatting | bytes 524288

commit v3 on v2

--- a/solution.py
+++ b/solution.py
@@ -97,13 +97,13 @@
 
 def fused_kernel(
     x_ref, q_hbm, k_hbm, v_hbm, o_hbm, do_hbm, lse_hbm, order_ref,
-    dq_ref, dw_ref,
-    q_ref, o_ref, do_ref, lse_ref, xbuf, kv, lse2, delta, dq_acc, own, acc, g_send, g_recv, g_mine, g_other,
+    dq_hbm, dw_ref,
+    dq_ref, q_ref, o_ref, do_ref, lse_ref, xbuf, kv, lse2, delta, dq_acc, own, acc, g_send, g_recv, g_mine, g_other,
     a_keep, b_keep, a1_send, a1_recv, b1_send, b1_recv,
     a2_send, a2_recv, b2_send, b2_recv, last_keep, last_send, last_recv,
     x_local, x_send, x_recv, kv_ssem, kv_rsem, g_ssem, g_rsem,
     a1_ssem, a1_rsem, b1_ssem, b1_rsem, a2_ssem, a2_rsem, b2_ssem, b2_rsem,
-    last_ssem, last_rsem, in_sem,
+    last_ssem, last_rsem, in_sem, dq_sem,
 ):
     rows, dh = k_hbm.shape[1], k_hbm.shape[2]
     heads = q_ref.shape[2] // dh
@@ -210,7 +210,7 @@
             )
 
         def one(h):
-            cols = pl.ds(pl.multiple_of(h * dh, dh), dh)
+            cols = pl.ds(h * dh, dh)
             query = q_ref[0, :, cols]
             grad = do_ref[0, :, cols]
             score = dot(keys, query, ((1,), (1,)))
@@ -229,11 +229,10 @@
                 dq_acc[h] += d_query
             return d_key, d_value
 
-        @pl.loop(0, heads // 4)
-        def _(group):
-            parts = [one(4 * group + i) for i in range(4)]
-            total[:, 0:dh] += (parts[0][0] + parts[1][0]) + (parts[2][0] + parts[3][0])
-            total[:, dh : 2 * dh] += (parts[0][1] + parts[1][1]) + (parts[2][1] + parts[3][1])
+        for h in range(heads):
+            d_key, d_value = one(h)
+            total[:, 0:dh] += d_key
+            total[:, dh : 2 * dh] += d_value
 
     def give(slot, peer):
         g_send[slot - 1, :, 0:dh] = (acc[:, 0:dh] * scale).astype(BF16)
@@ -257,7 +256,10 @@
     @pl.loop(0, heads)
     def _(h):
         cols = pl.ds(pl.multiple_of(h * dh, dh), dh)
-        dq_ref[0, :, cols] = (dq_acc[h] * scale).T.astype(BF16)
+        dq_ref[0, :, cols] = dq_acc[h].T
+
+    dq_copy = pltpu.make_async_copy(dq_ref, dq_hbm, dq_sem.at[0])
+    dq_copy.start()
 
     for copy in given:
         copy.wait_recv()
@@ -342,6 +344,7 @@
     for k in range(3):
         result = result + last_recv[k].astype(F32)
     dw_ref[...] = result.T
+    dq_copy.wait()
     for copy in started:
         copy.wait_send()
 
@@ -352,15 +355,16 @@
     wide = 2 * dh
     vmem = pl.BlockSpec(memory_space=pltpu.VMEM)
     dma = pltpu.SemaphoreType.DMA
-    return pl.pallas_call(
+    d_query, d_weight = pl.pallas_call(
         fused_kernel,
         out_shape=(
-            jax.ShapeDtypeStruct(query_rows.shape, BF16),
+            jax.ShapeDtypeStruct(query_rows.shape, F32),
             jax.ShapeDtypeStruct((rows, wide), F32),
         ),
         in_specs=[pl.BlockSpec(memory_space=pltpu.HBM)] * 7 + [pl.BlockSpec(memory_space=pltpu.SMEM)],
-        out_specs=(vmem, vmem),
+        out_specs=(pl.BlockSpec(memory_space=pltpu.HBM), vmem),
         scratch_shapes=[
+            pltpu.VMEM(query_rows.shape, F32),
             pltpu.VMEM(query_rows.shape, BF16),
             pltpu.VMEM(query_rows.shape, BF16),
             pltpu.VMEM(query_rows.shape, BF16),
@@ -393,7 +397,7 @@
             dma((3,)), dma((3,)), dma((4,)), dma((4,)),
             dma((4,)), dma((4,)), dma((4,)), dma((4,)),
             dma((4,)), dma((4,)), dma((4,)), dma((4,)),
-            dma((3,)), dma((3,)), dma((6,)),
+            dma((3,)), dma((3,)), dma((6,)), dma((1,)),
         ],
         compiler_params=pltpu.CompilerParams(
             collective_id=0, has_side_effects=True, vmem_limit_bytes=64 * 1024 * 1024
@@ -404,6 +408,7 @@
             transcendentals=4 * heads * rows * rows,
         ),
     )(layer_input, query_rows, key_rows, value_rows, attn_out, d_attn, log_sum_exp, block_order)
+    return (d_query * dh ** (-0.5)).astype(BF16), d_weight
 
 
 def fits(mesh):

time: 49.5 us -> 48.9 us (0.988)
  other arithmetic: 0 us -> 2.12 us
  local copies, waits for them, and re-layouts: 3.54 us -> 1.67 us
  Pallas kernels: 45.1 us -> 44.3 us
    convert_element_type x0 -> x1, other arithmetic: none -> 2.12 us  [fused_body(): return ((d_query * dh ** (-0.5)).astype(BF16), d_weight)]
    unnamed x2 -> x1, local copies, waits for them, and re-layouts: 3.54 us -> 1.67 us
    pallas_call x1, Pallas kernels: 45.1 us -> 44.3 us  [fused_body(): pl.pallas_call(fused_kernel, out_shape=(jax.ShapeDtypeStruct(query_rows.s...]
where the time goes in v3:
time: 48.9 us; the launch traced here: 48.7 us
  Pallas kernels  44.3 us (91%)
  other arithmetic  2.12 us (4%)
  local copies, waits for them, and re-layouts  1.67 us (3%)
  between operations  0.64 us (1%)
    pallas_call x1, Pallas kernels, fused_body(): pl.pallas_call(fused_kernel, out_shape=(jax.ShapeDtypeStruct(query_rows.s...  44.3 us
    convert_element_type x1, other arithmetic, fused_body(): return ((d_query * dh ** (-0.5)).astype(BF16), d_weight)  2.12 us
    unnamed x1, local copies, waits for them, and re-layouts  1.67 us

profile of v3, /device:TPU:0, one launch (start us, length us, event | category | flops | bytes accessed | tf_op | source)
XLA Modules:
  0.0 48.7 jit_solution(2543059079141597170)
XLA Ops:
  0.6 44.3 %shard_map.95 = (f32[1,256,1024]{2,1,0:T(8,128)}, f32[256,256]{1,0:T(8,128)}) custom-call(bf16[1,256,8192]{2,1,0:T(8,128)(2,1)} %x_ref.1, bf16[1,256,1024]{2,1,0:T(8,128)(2,1)} %q_hbm.1, bf16[1,256,128]{2,1,0:T(8,128)(2,1)} %k_hbm.1, bf16[1,256,128]{2,1,0:T(8,128)(2,1)} %v_hbm.1, bf16[1,256,1024]{2,1,0:T(8,128)(2,1)} %o_hbm.1, bf16[1,256,1024]{2,1,0:T(8,128)(2,1)} %do_hbm.1, ...), custom_call_target="tpu_custom_call" | custom-call | flops 3758096384 | bytes 8388608 | tf_op jit(solution)/shard_map/pallas_call | solution.py:358
  44.9 2.1 %multiply_convert_fusion = bf16[1,256,1024]{2,1,0:T(8,128)(2,1)} fusion(f32[1,256,1024]{2,1,0:T(8,128)} %get-tuple-element.4), kind=kLoop, calls=%fused_computation | loop fusion | flops 524288 | bytes 1572864 | tf_op jit(solution)/shard_map/convert_element_type | solution.py:411
  47.1 1.7 %copy.11 = f32[256,256]{1,0:T(8,128)} copy(f32[256,256]{1,0:T(8,128)} %get-tuple-element.9) | data formatting | bytes 524288

commit v4 on v3

--- a/solution.py
+++ b/solution.py
@@ -256,7 +256,7 @@
     @pl.loop(0, heads)
     def _(h):
         cols = pl.ds(pl.multiple_of(h * dh, dh), dh)
-        dq_ref[0, :, cols] = dq_acc[h].T
+        dq_ref[0, :, cols] = (dq_acc[h] * scale).T.astype(BF16)
 
     dq_copy = pltpu.make_async_copy(dq_ref, dq_hbm, dq_sem.at[0])
     dq_copy.start()
@@ -328,11 +328,11 @@
     s = STRIPS
     stage_one(s[0])
     stage_one(s[1])
+    stage_one(s[2])
     stage_two(s[0])
-    stage_one(s[2])
+    stage_one(s[3])
     stage_two(s[1])
     stage_three(s[0])
-    stage_one(s[3])
     stage_two(s[2])
     stage_three(s[1])
     stage_two(s[3])
@@ -355,16 +355,16 @@
     wide = 2 * dh
     vmem = pl.BlockSpec(memory_space=pltpu.VMEM)
     dma = pltpu.SemaphoreType.DMA
-    d_query, d_weight = pl.pallas_call(
+    return pl.pallas_call(
         fused_kernel,
         out_shape=(
-            jax.ShapeDtypeStruct(query_rows.shape, F32),
+            jax.ShapeDtypeStruct(query_rows.shape, BF16),
             jax.ShapeDtypeStruct((rows, wide), F32),
         ),
         in_specs=[pl.BlockSpec(memory_space=pltpu.HBM)] * 7 + [pl.BlockSpec(memory_space=pltpu.SMEM)],
         out_specs=(pl.BlockSpec(memory_space=pltpu.HBM), vmem),
         scratch_shapes=[
-            pltpu.VMEM(query_rows.shape, F32),
+            pltpu.VMEM(query_rows.shape, BF16),
             pltpu.VMEM(query_rows.shape, BF16),
             pltpu.VMEM(query_rows.shape, BF16),
             pltpu.VMEM(query_rows.shape, BF16),
@@ -408,7 +408,6 @@
             transcendentals=4 * heads * rows * rows,
         ),
     )(layer_input, query_rows, key_rows, value_rows, attn_out, d_attn, log_sum_exp, block_order)
-    return (d_query * dh ** (-0.5)).astype(BF16), d_weight
 
 
 def fits(mesh):

time: 48.9 us -> 51.1 us (1.045)
  Pallas kernels: 44.3 us -> 46.7 us
  other arithmetic: 2.12 us -> 0 us
  local copies, waits for them, and re-layouts: 1.67 us -> 3.54 us
    pallas_call x1, Pallas kernels: 44.3 us -> 46.7 us  [fused_body(): pl.pallas_call(fused_kernel, out_shape=(jax.ShapeDtypeStruct(query_rows.s...]
    convert_element_type x1 -> x0, other arithmetic: 2.12 us -> none  [fused_body(): return ((d_query * dh ** (-0.5)).astype(BF16), d_weight)]
    unnamed x1 -> x2, local copies, waits for them, and re-layouts: 1.67 us -> 3.54 us
where the time goes in v4:
time: 51.1 us; the launch traced here: 50.9 us
  Pallas kernels  46.7 us (91%)
  local copies, waits for them, and re-layouts  3.54 us (7%)
  between operations  0.64 us (1%)
    pallas_call x1, Pallas kernels, fused_body(): pl.pallas_call(fused_kernel, out_shape=(jax.ShapeDtypeStruct(query_rows.s...  46.7 us
    unnamed x2, local copies, waits for them, and re-layouts  3.54 us

profile of v4, /device:TPU:0, one launch (start us, length us, event | category | flops | bytes accessed | tf_op | source)
XLA Modules:
  0.0 50.9 jit_solution(7883947720608599199)
XLA Ops:
  0.6 46.7 %shard_map.95 = (bf16[1,256,1024]{2,1,0:T(8,128)(2,1)}, f32[256,256]{1,0:T(8,128)}) custom-call(bf16[1,256,8192]{2,1,0:T(8,128)(2,1)} %x_ref.1, bf16[1,256,1024]{2,1,0:T(8,128)(2,1)} %q_hbm.1, bf16[1,256,128]{2,1,0:T(8,128)(2,1)} %k_hbm.1, bf16[1,256,128]{2,1,0:T(8,128)(2,1)} %v_hbm.1, bf16[1,256,1024]{2,1,0:T(8,128)(2,1)} %o_hbm.1, ...), custom_call_target="tpu_custom_call" | custom-call | flops 3758096384 | bytes 8388608 | tf_op jit(solution)/shard_map/pallas_call | solution.py:358
  47.4 1.9 %copy.12 = bf16[1,256,1024]{2,1,0:T(8,128)(2,1)} copy(bf16[1,256,1024]{2,1,0:T(8,128)(2,1)} %get-tuple-element.4) | data formatting | bytes 1048576
  49.2 1.7 %copy.13 = f32[256,256]{1,0:T(8,128)} copy(f32[256,256]{1,0:T(8,128)} %get-tuple-element.5) | data formatting | bytes 524288
